TPU v7x, 32 devices: a whole 2x2x4 slice. The times are simulated.
32 devices in a mesh: ctx: 16 (over z, x, core), head: 2 (over y).
Axes of the slice: x: 2, y: 2, z: 4, core: 2. Of those that a mesh axis runs over, the one named last changes fastest.
Arguments:
- query_raw: bfloat16 [2048, 2048], P('ctx', 'head'), may hold values from -6 to 6
- key_raw: bfloat16 [2048, 2048], P('ctx', 'head'), may hold values from -6 to 6
- value_raw: bfloat16 [2048, 4096], P('ctx', 'head'), may hold values from -6 to 6
- query_key_conv: bfloat16 [2, 4, 2048], P(None, None, 'head'), may hold values from -3 to 3
- value_conv: bfloat16 [4, 4096], P(None, 'head'), may hold values from -3 to 3
- output_gate: bfloat16 [2048, 4096], P('ctx', 'head'), may hold values from -6 to 6
- beta_logit: float32 [2048, 32], P('ctx', 'head')
- gate_logit: float32 [2048, 32], P('ctx', 'head')
- log_rate: float32 [32], P('head')
- norm_gain: float32 [128], replicated, may hold values from 0.5 to 2
- out_weight: bfloat16 [4096, 2048], P('head'), may hold values from -0.09375 to 0.09375
Outputs:
- mixed: bfloat16 [2048, 2048], P(('ctx', 'head'))
All inputs are finite; a program needn't handle non-finite values.
Results may differ from a plain program's by a relative error of at most 0.022.
Values may be sent and summed in bfloat16 or wider, within the bound.
A program may use at most 128 MiB of HBM per device.

v0:
```python
import jax
import jax.numpy as jnp
from jax import lax
from jax.sharding import PartitionSpec as P

HDIM = 128
CONV = 4
SPAN = 128


def from_behind(value, axis, by):
    devices = lax.axis_size(axis)
    pairs = [(i, i + by) for i in range(devices) if 0 <= i + by < devices]
    return lax.ppermute(value, axis, pairs)


def prefix_2(value, axis, join, neutral):
    place = lax.axis_index(axis)
    gathered = jax.tree.map(
        lambda a, kind: lax.all_gather(a.astype(kind), axis), value, (jnp.bfloat16, jnp.bfloat16)
    )
    state = jax.tree.map(lambda a, e: jnp.zeros_like(a) + jnp.asarray(e, a.dtype), value, neutral)

    def one(lap, state):
        return join(
            state,
            jax.tree.map(
                lambda a, own: lax.dynamic_index_in_dim(a, lap, 0, False).astype(own.dtype),
                gathered,
                value,
            ),
        )

    return lax.fori_loop(0, place, one, state)


def conv_block(raw_rows, rim_rows, taps):
    length = raw_rows.shape[0]
    extended = jnp.concatenate([rim_rows, raw_rows], axis=0).astype(jnp.float32)
    total = jnp.zeros((length, raw_rows.shape[1]), jnp.float32)
    for offset in range(CONV):
        total = total + taps[offset].astype(jnp.float32) * extended[offset : offset + length]
    return jax.nn.silu(total)


def unit_rows(values):
    return values / jnp.sqrt(jnp.sum(values * values, axis=-1, keepdims=True) + 1e-06)


def local(
    query_raw,
    key_raw,
    value_raw,
    query_key_conv,
    value_conv,
    output_gate,
    beta_logit,
    gate_logit,
    log_rate,
    norm_gain,
    out_weight,
):
    highest_precision = lax.Precision.HIGHEST
    length = query_raw.shape[0]
    qk_width = query_raw.shape[1]
    v_width = value_raw.shape[1]
    key_heads = qk_width // HDIM
    value_heads = v_width // HDIM
    ratio = value_heads // key_heads
    blocks = length // SPAN
    keep = CONV - 1
    rim_rows = jnp.concatenate(
        [query_raw[length - keep :], key_raw[length - keep :], value_raw[length - keep :]], axis=1
    )
    earlier = from_behind(rim_rows, "ctx", 1)
    query = conv_block(query_raw, earlier[:, :qk_width], query_key_conv[0]).reshape(
        length, key_heads, HDIM
    )
    keyed = conv_block(key_raw, earlier[:, qk_width : 2 * qk_width], query_key_conv[1]).reshape(
        length, key_heads, HDIM
    )
    value = conv_block(value_raw, earlier[:, 2 * qk_width :], value_conv).reshape(
        length, value_heads, HDIM
    )
    query = jnp.repeat(unit_rows(query) * HDIM ** (-0.5), ratio, axis=1)
    keyed = jnp.repeat(unit_rows(keyed), ratio, axis=1)
    beta = jax.nn.sigmoid(beta_logit)
    decay = -jnp.exp(log_rate)[None, :] * jax.nn.softplus(gate_logit)

    def to_blocks(values):
        return values.reshape(blocks, SPAN, value_heads, HDIM).transpose(2, 0, 1, 3)

    query_blk = to_blocks(query)
    key_blk = to_blocks(keyed)
    value_blk = to_blocks(value)
    beta_blk = beta.reshape(blocks, SPAN, value_heads).transpose(2, 0, 1)
    gamma = jnp.cumsum(decay.reshape(blocks, SPAN, value_heads).transpose(2, 0, 1), axis=-1)
    relative = gamma[..., :, None] - gamma[..., None, :]
    position_list = jnp.arange(SPAN)
    below = position_list[:, None] > position_list[None, :]
    upto = position_list[:, None] >= position_list[None, :]
    strict_decay = jnp.where(below, jnp.exp(jnp.where(below, relative, 0.0)), 0.0)
    within_decay = jnp.where(upto, jnp.exp(jnp.where(upto, relative, 0.0)), 0.0)
    key_key = jnp.einsum("hncd,hnsd->hncs", key_blk, key_blk, precision=highest_precision)
    lower_part = strict_decay * key_key * beta_blk[..., None, :]
    system = jnp.eye(SPAN, dtype=jnp.float32) + lower_part
    growth = jnp.exp(gamma)[..., None]
    right_side = jnp.concatenate([value_blk, growth * key_blk], axis=-1)
    solved = lax.linalg.triangular_solve(
        system, right_side, left_side=True, lower=True, unit_diagonal=True
    )
    fresh = solved[..., :HDIM]
    wy_keys = solved[..., HDIM:]
    query_key = jnp.einsum("hncd,hnsd->hncs", query_blk, key_blk, precision=highest_precision)
    scores = within_decay * query_key * beta_blk[..., None, :]
    local_out = jnp.einsum("hncs,hnsv->hncv", scores, fresh, precision=highest_precision)
    lifted = growth * query_blk - jnp.einsum(
        "hncs,hnsk->hnck", scores, wy_keys, precision=highest_precision
    )
    tail_weight = (jnp.exp(gamma[..., -1:] - gamma) * beta_blk)[..., None] * key_blk
    identity_map = jnp.eye(HDIM, dtype=jnp.float32)
    transition = jnp.exp(gamma[..., -1])[..., None, None] * identity_map - jnp.einsum(
        "hnck,hncj->hnkj", tail_weight, wy_keys, precision=highest_precision
    )
    pushed = jnp.einsum("hnck,hncv->hnkv", tail_weight, fresh, precision=highest_precision)

    def matmul(left, right):
        return jnp.einsum("hij,hjk->hik", left, right, precision=highest_precision)

    def compose(carried, item):
        product, memory_state = carried
        step_map, step_push = item
        return (
            (matmul(step_map, product), matmul(step_map, memory_state) + step_push),
            (product, memory_state),
        )

    start_map = jnp.broadcast_to(identity_map, (value_heads, HDIM, HDIM))
    start_state = jnp.zeros((value_heads, HDIM, HDIM), jnp.float32)
    block_items = (transition.transpose(1, 0, 2, 3), pushed.transpose(1, 0, 2, 3))
    (shard_map_total, shard_state), (maps_before, states_before) = lax.scan(
        compose, (start_map, start_state), block_items
    )

    def combine(first, second):
        return (matmul(second[0], first[0]), matmul(second[0], first[1]) + second[1])

    prefix = prefix_2((shard_map_total, shard_state), "ctx", combine, (start_map, start_state))

    def sweep(memory_state, item):
        raised_block, block_local, step_map, step_push = item
        layer_output = block_local + jnp.einsum(
            "msq,mqz->msz", raised_block, memory_state, precision=highest_precision
        )
        return (matmul(step_map, memory_state) + step_push, layer_output)

    sweep_items = (
        lifted.transpose(1, 0, 2, 3),
        local_out.transpose(1, 0, 2, 3),
        block_items[0],
        block_items[1],
    )
    _, outputs = lax.scan(sweep, prefix[1], sweep_items)
    core = outputs.transpose(1, 0, 2, 3)
    core = core.transpose(1, 2, 0, 3).reshape(length, value_heads, HDIM)
    meansq = jnp.mean(core * core, axis=-1, keepdims=True)
    gate = jax.nn.silu(output_gate.reshape(length, value_heads, HDIM).astype(jnp.float32))
    normed = (
        (core / jnp.sqrt(meansq + 1e-06) * norm_gain * gate)
        .astype(jnp.bfloat16)
        .reshape(length, v_width)
    )
    return lax.psum_scatter(
        jnp.dot(normed, out_weight, preferred_element_type=jnp.float32).astype(jnp.bfloat16),
        "head",
        scatter_dimension=0,
        tiled=True,
    )


def solution(mesh):
    in_specs = (
        P("ctx", "head"),
        P("ctx", "head"),
        P("ctx", "head"),
        P(None, None, "head"),
        P(None, "head"),
        P("ctx", "head"),
        P("ctx", "head"),
        P("ctx", "head"),
        P("head"),
        P(),
        P("head", None),
    )
    out_specs = P(("ctx", "head"), None)
    return jax.shard_map(local, mesh=mesh, in_specs=in_specs, out_specs=out_specs, check_vma=False)
```

profile of v0, /device:TPU:24, one launch (start us, length us, event | category | flops | bytes accessed | tf_op | source)
XLA Modules:
  0.0 405.5 jit_solution(14766721588629947708)
XLA Ops:
  21.4 2.5 divide_multiply_fusion
  25.3 2.5 fusion.12
  27.8 157.8 %custom-call.3 = f32[16,1,1,128,128]{3,4,2,1,0:T(8,128)} custom-call(f32[16,1,1,128,128]{4,3,2,1,0:T(8,128)S(1)} %fusion.12), custom_call_target="InvertDiagBlocksLowerTriangular" | custom-call | tf_op jit(solution)/shard_map/triangular_solve | solution.py:109
  189.5 2.0 convolution_subtract_fusion
  194.6 2.3 fusion.41
  196.9 2.7 fusion.15
  199.7 2.0 copy.45
  203.0 2.3 fusion.8
  205.4 2.2 fusion.14
  207.6 2.9 fusion.33
  210.5 58.4 %all-gather.5.cloned.1.call-done = bf16[256,128,128]{2,1,0:T(8,128)(2,1)} async-done(((bf16[16,128,128]{2,1,0:T(8,128)(2,1)}), bf16[256,128,128]{2,1,0:T(8,128)(2,1)}) %all-gather.5.cloned.1.call-update) | async-done | bytes 8388624 | tf_op jit(solution)/shard_map/all_gather | solution.py:20
  268.9 75.3 %all-gather.7.cloned.1.call-done = bf16[256,128,128]{2,1,0:T(8,128)(2,1)} async-done(((bf16[16,128,128]{2,1,0:T(8,128)(2,1)}), bf16[256,128,128]{2,1,0:T(8,128)(2,1)}) %all-gather.7.cloned.1.call-update) | async-done | bytes 8388624 | tf_op jit(solution)/shard_map/all_gather | solution.py:20
  344.4 24.8 %while.3 = (s32[]{:T(128)}, f32[16,128,128]{2,1,0:T(8,128)S(1)}, s32[]{:T(128)}, bf16[16,16,128,128]{3,2,1,0:T(8,128)(2,1)}, bf16[16,16,128,128]{3,2,1,0:T(8,128)(2,1)}, /*index=5*/s32[]{:T(128)}, s32[]{:T(128)}, s32[]{:T(128)}) while((s32[]{:T(128)}, f32[16,128,128]{2,1,0:T(8,128)S(1)}, s32[]{:T(128)}, bf16[16,16,128,128]{3,2,1,0:T(8,128)(2,1)}, ...), condition=%wide.region_4.5_spmd, body=%wide.region_3.4_spmd.sunk | while | flops 403177472 | bytes 5244031 | solution.py:34
  344.5 2.0 convolution_add_fusion.4
  346.6 1.9 convolution_add_fusion.4
  348.6 1.9 convolution_add_fusion.4
  352.7 1.9 convolution_add_fusion.4
  354.7 1.9 convolution_add_fusion.4
  356.7 1.9 convolution_add_fusion.4
  360.8 1.9 convolution_add_fusion.4
  366.9 1.9 convolution_add_fusion.4
  369.1 3.2 fusion.28
  372.8 5.5 %convolution_convert_fusion = bf16[128,2048]{1,0:T(8,128)(2,1)} fusion(bf16[128,2048]{0,1:T(8,128)(2,1)S(1)} %fusion.32, bf16[2048,2048]{1,0:T(8,128)(2,1)} %param.23), kind=kOutput, calls=%fused_computation.4 | convolution fusion | flops 1074003968 | bytes 9437184 | tf_op jit(solution)/shard_map/dot_general | solution.py:174
  378.3 20.7 %reduce-scatter.2.cloned.1.call-done = bf16[64,2048]{1,0:T(8,128)(2,1)} async-done(((bf16[128,2048]{1,0:T(8,128)(2,1)}), bf16[64,2048]{1,0:T(8,128)(2,1)}) %reduce-scatter.2.cloned.1.call-update) | async-done | bytes 262160 | tf_op jit(solution)/shard_map/reduce_scatter | solution.py:173
  (90 shorter events, 33.3 us)
Async XLA Ops:
  6.5 195.2 %copy-start = (f32[128]{0:T(128)S(1)}, f32[128]{0:T(128)}, u32[]{:S(2)}) copy-start(f32[128]{0:T(128)} %param.22) | copy-start | bytes 1540
  6.5 262.4 %all-gather.5.cloned.1.call-start = ((), (), s32[]{:S(2)}) async-start(), calls=%async_computation.2 | async-start | bytes 8912896 | tf_op jit(solution)/shard_map/all_gather | solution.py:20
  8.8 8.6 %collective-permute-start = (bf16[3,4096]{1,0:T(4,128)(2,1)S(1)}, bf16[3,4096]{1,0:T(4,128)(2,1)S(1)}, u32[]{:S(2)}, u32[]{:S(2)}) collective-permute-start(bf16[3,4096]{1,0:T(4,128)(2,1)S(1)} %pad_maximum_fusion), channel_id=1, source_target_pairs={{0,2},{2,4},{4,6},{6,8},{8,10},{10,12},{12,14},{14,16},{16,18},{18... | collective-permute-start | bytes 73736 | tf_op jit(solution)/shard_map/ppermute | solution.py:14
  19.6 166.0 %copy-start.4 = (f32[128,8,128]{2,0,1:T(8,128)}, f32[128,8,128]{2,0,1:T(8,128)S(1)}, u32[]{:S(2)}) copy-start(f32[128,8,128]{2,0,1:T(8,128)S(1)} %copy.35) | copy-start | bytes 1572868
  185.6 1.5 copy-start.5
  185.6 1.9 copy-start.9
  187.1 2.4 copy-start.1
  191.5 1.0 copy-start.3
  194.3 149.9 %all-gather.7.cloned.1.call-start = ((), (), s32[]{:S(2)}) async-start(), calls=%async_computation.3 | async-start | bytes 8912896 | tf_op jit(solution)/shard_map/all_gather | solution.py:20
  194.6 2.3 copy-start.2
  199.7 199.3 %reduce-scatter.2.cloned.1.call-start = ((), (), s32[]{:S(2)}) async-start(), calls=%async_computation.1 | async-start | bytes 786432 | tf_op jit(solution)/shard_map/reduce_scatter | solution.py:173
  201.8 3.6 copy-start.7
  344.3 24.8 %copy-start.6 = (f32[16,128,128]{1,2,0:T(8,128)S(1)}, f32[16,128,128]{1,2,0:T(8,128)}, u32[]{:S(2)}) copy-start(f32[16,128,128]{1,2,0:T(8,128)} %fusion.33) | copy-start | bytes 3145732
  369.1 3.2 copy-start.8
Sparse Core Ops, SparseCore 0:
  194.5 74.3 all-gather.4
  271.1 73.1 all-gather.6
  378.4 20.5 reduce-scatter.1
where the time goes:
time: 408 us; the launch traced here: 406 us
  other arithmetic  170 us (42%)
  waiting for transfers between devices  155 us (38%)
  matrix products  52.6 us (13%)
  between operations  13.5 us (3%)
  local copies, waits for them, and re-layouts  11.5 us (3%)
    another operation x2, other arithmetic, local(): lax.linalg.triangular_solve(system, right_side, left_side=True, lower=Tru...  158 us
    all_gather x2, waiting for transfers between devices, prefix_2(): lax.all_gather(a.astype(kind), axis)  134 us
    dot_general x14, matrix products, matmul(): return jnp.einsum('hij,hjk->hik', left, right, precision=highest_precision)  27.3 us
    reduce_scatter x1, waiting for transfers between devices, local(): lax.psum_scatter(jnp.dot(normed, out_weight, preferred_element_type=jnp.f...  20.7 us
  transfers between devices with their start and end apart: 4, of which 3 were waited for; matrix products, arithmetic and copies ran while one was open for 6% of the time, Pallas kernels for 0%

commit v1 on v0

v1 whole, which is shorter than its diff:
```python
import functools

import jax
import jax.numpy as jnp
from jax import lax
from jax.experimental import pallas as pl
from jax.experimental.pallas import tpu as pltpu
from jax.sharding import PartitionSpec as P

HDIM = 128
CONV = 4
RIM = 16
MESH = pl.DeviceIdType.MESH
F32 = jnp.float32
BF16 = jnp.bfloat16


def mm(left, right):
    return jnp.dot(left.astype(BF16), right.astype(BF16), preferred_element_type=F32)


def mm_exact(left, right):
    return jnp.dot(left, right, precision=lax.Precision.HIGHEST, preferred_element_type=F32)


def silu(values):
    return values / (1.0 + jnp.exp(-values))


def unit_inverse(lower, row, col):
    pair = ((row ^ 1) == col) & (col < row)
    inverse = jnp.where(row == col, 1.0, 0.0) - jnp.where(pair, lower, 0.0)
    size = 2
    while size < lower.shape[0]:
        mask = (row // (2 * size) == col // (2 * size)) & (row // size > col // size)
        narrow = inverse.astype(BF16)
        step = mm(jnp.where(mask, lower, 0.0), narrow)
        inverse = inverse - mm(narrow, step)
        size *= 2
    return inverse


def layer_kernel(
    n_ctx,
    n_head,
    q_ref,
    k_ref,
    v_ref,
    qk_taps_ref,
    v_taps_ref,
    gate_ref,
    beta_ref,
    rate_ref,
    log_rate_ref,
    gain_ref,
    w_hbm,
    out_ref,
    ext,
    rim_q,
    rim_k,
    rim_v,
    taps,
    square,
    gamma_rows,
    beta_rows,
    map_ref,
    push_ref,
    lift_ref,
    local_ref,
    last_ref,
    state_in,
    state_out,
    total,
    part,
    part_in,
    w_ref,
    w_sem,
    rim_send,
    rim_recv,
    state_send,
    state_recv,
    part_send,
    part_recv,
):
    ctx = lax.axis_index("ctx")
    head = lax.axis_index("head")
    length = q_ref.shape[0]
    qk_width = q_ref.shape[1]
    v_width = v_ref.shape[1]
    heads = v_width // HDIM
    ratio = v_width // qk_width
    rows_out = length // n_head
    has_next = ctx < n_ctx - 1
    has_prev = ctx > 0
    after = jnp.minimum(ctx + 1, n_ctx - 1)
    before = jnp.maximum(ctx - 1, 0)

    w_copy = pltpu.make_async_copy(w_hbm, w_ref, w_sem)
    w_copy.start()

    barrier = pltpu.get_barrier_semaphore()

    @pl.when(has_next)
    def _():
        pl.semaphore_signal(barrier, inc=1, device_id=(after, head), device_id_type=MESH)

    @pl.when(has_prev)
    def _():
        pl.semaphore_signal(barrier, inc=1, device_id=(before, head), device_id_type=MESH)

    for hop in range(1, n_head):
        peer = lax.rem(head + hop, n_head)
        pl.semaphore_signal(barrier, inc=1, device_id=(ctx, peer), device_id_type=MESH)

    neighbours = has_next.astype(jnp.int32) + has_prev.astype(jnp.int32) + (n_head - 1)
    pl.semaphore_wait(barrier, neighbours)

    rims = [
        pltpu.make_async_remote_copy(
            src_ref=src.at[pl.ds(length - RIM, RIM), :],
            dst_ref=dst,
            send_sem=rim_send.at[i],
            recv_sem=rim_recv.at[i],
            device_id=(after, head),
            device_id_type=MESH,
        )
        for i, (src, dst) in enumerate(((q_ref, rim_q), (k_ref, rim_k), (v_ref, rim_v)))
    ]

    @pl.when(has_next)
    def _():
        for copy in rims:
            copy.start()

    row = lax.broadcasted_iota(jnp.int32, (HDIM, HDIM), 0)
    col = lax.broadcasted_iota(jnp.int32, (HDIM, HDIM), 1)
    rate = rate_ref[...]
    soft = jnp.maximum(rate, 0.0) + jnp.log1p(jnp.exp(-jnp.abs(rate)))
    square[...] = jnp.zeros_like(square)
    square[:, 0:heads] = -jnp.exp(log_rate_ref[...]) * soft
    upper = jnp.where(row <= col, 1.0, 0.0)
    gamma_rows[...] = mm_exact(square[...].T, upper)
    square[:, 0:heads] = 1.0 / (1.0 + jnp.exp(-beta_ref[...]))
    beta_rows[...] = square[...].T
    taps[:, 0:qk_width] = qk_taps_ref[0].astype(F32)
    taps[:, qk_width : 2 * qk_width] = qk_taps_ref[1].astype(F32)
    taps[:, 2 * qk_width :] = v_taps_ref[...].astype(F32)
    spans = ((q_ref, rim_q, 0), (k_ref, rim_k, qk_width), (v_ref, rim_v, 2 * qk_width))
    for ref, _, start in spans:
        ext[8 : 8 + length, start : start + ref.shape[1]] = ref[...].astype(F32)

    @pl.when(has_prev)
    def _():
        for copy in rims:
            copy.wait_recv()
        for _, rim, start in spans:
            ext[0:8, start : start + rim.shape[1]] = rim[...].astype(F32)[RIM - 8 : RIM]

    @pl.when(jnp.logical_not(has_prev))
    def _():
        ext[0:8, :] = jnp.zeros((8, ext.shape[1]), F32)

    def conv(start):
        at = pl.ds(pl.multiple_of(start, HDIM), HDIM)
        result = taps[0:1, at] * ext[5 : 5 + length, at]
        for offset in range(1, CONV):
            result += taps[offset : offset + 1, at] * ext[5 + offset : 5 + offset + length, at]
        return silu(result)

    def unit(values):
        return values * lax.rsqrt(jnp.sum(values * values, axis=-1, keepdims=True) + 1e-06)

    key_group = 2 if (heads // ratio) % 2 == 0 else 1

    def local_step(group, _):
        for own in range(key_group):
            key_head = group * key_group + own
            query = unit(conv(key_head * HDIM)) * HDIM ** (-0.5)
            key = unit(conv(qk_width + key_head * HDIM))
            key_t = key.T
            key_key = mm(key, key_t)
            query_key = mm(query, key_t)
            for sub in range(ratio):
                h = key_head * ratio + sub
                value = conv(2 * qk_width + h * HDIM)
                gamma_r = gamma_rows[pl.ds(h, 1), :]
                beta_r = beta_rows[pl.ds(h, 1), :]
                gamma_c = jnp.broadcast_to(gamma_r, (HDIM, HDIM)).T
                upto = row >= col
                ratio_decay = jnp.exp(jnp.where(upto, gamma_c - gamma_r, 0.0)) * beta_r
                lower = jnp.where(row > col, ratio_decay * key_key, 0.0)
                scores = jnp.where(upto, ratio_decay * query_key, 0.0)
                growth = jnp.exp(gamma_c)
                inverse = unit_inverse(lower, row, col)
                solved = mm(inverse, jnp.concatenate([value, growth * key], axis=1))
                solved = solved.astype(BF16)
                raised = mm(scores, solved)
                last = gamma_c[HDIM - 1 : HDIM, :]
                tail = key_t * (jnp.exp(last - gamma_r) * beta_r)
                pushed = mm(tail, solved)
                map_ref[h] = pushed[:, HDIM:].astype(BF16)
                push_ref[h] = pushed[:, :HDIM]
                lift_ref[h] = (growth * query - raised[:, HDIM:]).astype(BF16)
                local_ref[h] = raised[:, :HDIM]
                last_ref[pl.ds(h, 1), :] = jnp.exp(last)
        return 0

    lax.fori_loop(0, heads // ratio // key_group, local_step, 0)

    @pl.when(jnp.logical_not(has_prev))
    def _():
        state_in[...] = jnp.zeros_like(state_in)

    total[...] = jnp.zeros_like(total)
    w_copy.wait()

    def state_copy(h):
        return pltpu.make_async_remote_copy(
            src_ref=state_out.at[h],
            dst_ref=state_in.at[h],
            send_sem=state_send.at[h],
            recv_sem=state_recv.at[h],
            device_id=(after, head),
            device_id_type=MESH,
        )

    def normed_head(h):
        @pl.when(has_prev)
        def _():
            state_copy(h).wait_recv()

        before_state = state_in[h]

        @pl.when(has_next)
        def _():
            moved = jnp.dot(map_ref[h], before_state, preferred_element_type=F32)
            grown = last_ref[pl.ds(h, 1), :] * before_state.astype(F32)
            state_out[h] = (grown - moved + push_ref[h]).astype(BF16)
            state_copy(h).start()

        core = local_ref[h] + jnp.dot(lift_ref[h], before_state, preferred_element_type=F32)
        scale = lax.rsqrt(jnp.mean(core * core, axis=-1, keepdims=True) + 1e-06)
        at = pl.ds(pl.multiple_of(h * HDIM, HDIM), HDIM)
        gate = silu(gate_ref[:, at].astype(F32))
        return (core * scale * gain_ref[...] * gate).astype(BF16)

    pairs = heads // 2

    def pair_rows(pair):
        return pl.ds(pl.multiple_of(pair * (2 * HDIM), 2 * HDIM), 2 * HDIM)

    def sweep(pair, _):
        normed = jnp.concatenate([normed_head(2 * pair), normed_head(2 * pair + 1)], axis=1)
        total[...] += jnp.dot(normed, w_ref[pair_rows(pair), :], preferred_element_type=F32)
        return 0

    lax.fori_loop(0, pairs, sweep, 0)
    part[...] = total[...].astype(BF16)

    copies = []
    for hop in range(1, n_head):
        peer = lax.rem(head + hop, n_head)
        copy = pltpu.make_async_remote_copy(
            src_ref=part.at[pl.ds(pl.multiple_of(peer * rows_out, 16), rows_out), :],
            dst_ref=part_in.at[hop - 1],
            send_sem=part_send.at[hop - 1],
            recv_sem=part_recv.at[hop - 1],
            device_id=(ctx, peer),
            device_id_type=MESH,
        )
        copy.start()
        copies.append(copy)
    mixed = part[pl.ds(pl.multiple_of(head * rows_out, 16), rows_out), :].astype(F32)
    for hop, copy in enumerate(copies):
        copy.wait_recv()
        mixed += part_in[hop].astype(F32)
    out_ref[...] = mixed.astype(BF16)

    for copy in copies:
        copy.wait_send()

    @pl.when(has_next)
    def _():
        for copy in rims:
            copy.wait_send()

        def drain(h, _):
            state_copy(h).wait_send()
            return 0

        lax.fori_loop(0, heads, drain, 0)


def local(n_ctx, n_head, *args):
    (q, k, v, qk_taps, v_taps, gate, beta, rate, log_rate, gain, weight) = args
    length, qk_width = q.shape
    v_width = v.shape[1]
    heads = v_width // HDIM
    model = weight.shape[1]
    rows_out = length // n_head
    width = 2 * qk_width + v_width
    vmem = pl.BlockSpec(memory_space=pltpu.VMEM)
    dma = pltpu.SemaphoreType.DMA
    blocks = (heads, HDIM, HDIM)
    peers = max(n_head - 1, 1)
    return pl.pallas_call(
        functools.partial(layer_kernel, n_ctx, n_head),
        out_shape=jax.ShapeDtypeStruct((rows_out, model), BF16),
        in_specs=[vmem] * 10 + [pl.BlockSpec(memory_space=pl.ANY)],
        out_specs=vmem,
        scratch_shapes=[
            pltpu.VMEM((8 + length, width), F32),
            pltpu.VMEM((RIM, qk_width), BF16),
            pltpu.VMEM((RIM, qk_width), BF16),
            pltpu.VMEM((RIM, v_width), BF16),
            pltpu.VMEM((CONV, width), F32),
            pltpu.VMEM((HDIM, HDIM), F32),
            pltpu.VMEM((HDIM, HDIM), F32),
            pltpu.VMEM((HDIM, HDIM), F32),
            pltpu.VMEM(blocks, BF16),
            pltpu.VMEM(blocks, F32),
            pltpu.VMEM(blocks, BF16),
            pltpu.VMEM(blocks, F32),
            pltpu.VMEM((heads, HDIM), F32),
            pltpu.VMEM(blocks, BF16),
            pltpu.VMEM(blocks, BF16),
            pltpu.VMEM((length, model), F32),
            pltpu.VMEM((length, model), BF16),
            pltpu.VMEM((peers, rows_out, model), BF16),
            pltpu.VMEM(weight.shape, BF16),
            dma,
            dma((3,)),
            dma((3,)),
            dma((heads,)),
            dma((heads,)),
            dma((peers,)),
            dma((peers,)),
        ],
        compiler_params=pltpu.CompilerParams(
            collective_id=0, has_side_effects=True, vmem_limit_bytes=48 * 2**20
        ),
    )(q, k, v, qk_taps, v_taps, gate, beta, rate, log_rate[None, :], gain[None, :], weight)


def solution(mesh):
    in_specs = (
        P("ctx", "head"),
        P("ctx", "head"),
        P("ctx", "head"),
        P(None, None, "head"),
        P(None, "head"),
        P("ctx", "head"),
        P("ctx", "head"),
        P("ctx", "head"),
        P("head"),
        P(),
        P("head", None),
    )
    out_specs = P(("ctx", "head"), None)
    return jax.shard_map(
        functools.partial(local, mesh.shape["ctx"], mesh.shape["head"]),
        mesh=mesh,
        in_specs=in_specs,
        out_specs=out_specs,
        check_vma=False,
    )
```

time: 408 us -> 84.2 us (0.21)
  the two profiles are of different devices: /device:TPU:24 before, /device:TPU:27 now
where the time goes in v1:
time: 84.2 us; the launch traced here: 83.8 us
  Pallas kernels  74.7 us (89%)
  local copies, waits for them, and re-layouts  9.02 us (11%)
    pallas_call x1, Pallas kernels, local(): pl.pallas_call(functools.partial(layer_kernel, n_ctx, n_head), out_shape=...  74.7 us
    unnamed x19, local copies, waits for them, and re-layouts  9.02 us

profile of v1, /device:TPU:27, one launch (start us, length us, event | category | flops | bytes accessed | tf_op | source)
XLA Modules:
  0.0 83.8 jit_solution(7302674567227781398)
XLA Ops:
  0.0 0.8 copy.12.beta_ref
  0.8 0.8 copy.13.rate_ref
  1.6 0.0 copy-start
  1.6 1.0 %copy-done = bf16[128,2048]{1,0:T(8,128)(2,1)S(1)} copy-done((bf16[128,2048]{1,0:T(8,128)(2,1)S(1)}, bf16[128,2048]{1,0:T(8,128)(2,1)}, u32[]{:S(2)}) %copy-start) | copy-done | bytes 524312
  2.6 0.0 copy-start.1
  2.6 1.0 %copy-done.1 = bf16[128,2048]{1,0:T(8,128)(2,1)S(1)} copy-done((bf16[128,2048]{1,0:T(8,128)(2,1)S(1)}, bf16[128,2048]{1,0:T(8,128)(2,1)}, u32[]{:S(2)}) %copy-start.1) | copy-done | bytes 524312
  3.7 0.0 copy-start.2
  3.7 0.9 %copy-done.2 = bf16[128,1024]{1,0:T(8,128)(2,1)S(1)} copy-done((bf16[128,1024]{1,0:T(8,128)(2,1)S(1)}, bf16[128,1024]{1,0:T(8,128)(2,1)}, u32[]{:S(2)}) %copy-start.2) | copy-done | bytes 262168
  4.6 0.0 copy-start.3
  4.6 0.9 %copy-done.3 = bf16[128,1024]{1,0:T(8,128)(2,1)S(1)} copy-done((bf16[128,1024]{1,0:T(8,128)(2,1)S(1)}, bf16[128,1024]{1,0:T(8,128)(2,1)}, u32[]{:S(2)}) %copy-start.3) | copy-done | bytes 262168
  5.6 0.0 copy-start.4
  5.6 0.7 copy-done.4
  6.3 0.0 copy-start.5
  6.3 0.7 copy-done.5
  7.0 0.0 copy-start.6
  7.0 0.7 copy-done.6
  7.7 0.0 copy-start.7
  7.7 0.7 copy-done.7
  8.3 74.7 %shard_map.109 = bf16[64,2048]{1,0:T(8,128)(2,1)S(1)} custom-call(bf16[128,1024]{1,0:T(8,128)(2,1)S(1)} %copy-done.2, bf16[128,1024]{1,0:T(8,128)(2,1)S(1)} %copy-done.3, bf16[128,2048]{1,0:T(8,128)(2,1)S(1)} %copy-done, bf16[2,4,1024]{2,1,0:T(4,128)(2,1)S(1)} %copy-done.4, bf16[4,2048]{1,0:T(4,128)(2,1)S(1)} %copy-done.5, bf16[128,2048]{1,0:T(8,128)(2,1)S(1)} %copy-done.1, ...), custom_call_target="tpu_custom_call" | custom-call | tf_op jit(solution)/shard_map/pallas_call | solution.py:306
  83.0 0.7 copy.15
Async XLA Ops:
  1.6 1.0 %copy-start = (bf16[128,2048]{1,0:T(8,128)(2,1)S(1)}, bf16[128,2048]{1,0:T(8,128)(2,1)}, u32[]{:S(2)}) copy-start(bf16[128,2048]{1,0:T(8,128)(2,1)} %v_ref.1) | copy-start | bytes 1572868
  2.6 1.0 %copy-start.1 = (bf16[128,2048]{1,0:T(8,128)(2,1)S(1)}, bf16[128,2048]{1,0:T(8,128)(2,1)}, u32[]{:S(2)}) copy-start(bf16[128,2048]{1,0:T(8,128)(2,1)} %gate_ref.1) | copy-start | bytes 1572868
  3.7 0.9 %copy-start.2 = (bf16[128,1024]{1,0:T(8,128)(2,1)S(1)}, bf16[128,1024]{1,0:T(8,128)(2,1)}, u32[]{:S(2)}) copy-start(bf16[128,1024]{1,0:T(8,128)(2,1)} %q_ref.1) | copy-start | bytes 786436
  4.6 0.9 %copy-start.3 = (bf16[128,1024]{1,0:T(8,128)(2,1)S(1)}, bf16[128,1024]{1,0:T(8,128)(2,1)}, u32[]{:S(2)}) copy-start(bf16[128,1024]{1,0:T(8,128)(2,1)} %k_ref.1) | copy-start | bytes 786436
  5.6 0.7 copy-start.4
  6.3 0.7 copy-start.5
  7.0 0.7 copy-start.6
  7.7 0.7 copy-start.7

commit v2 on v1

v2 whole, which is shorter than its diff:
```python
import functools

import jax
import jax.numpy as jnp
from jax import lax
from jax.experimental import pallas as pl
from jax.experimental.pallas import tpu as pltpu
from jax.sharding import PartitionSpec as P

HDIM = 128
CONV = 4
RIM = 16
MESH = pl.DeviceIdType.MESH
F32 = jnp.float32
BF16 = jnp.bfloat16


def mm(left, right):
    return jnp.dot(left.astype(BF16), right.astype(BF16), preferred_element_type=F32)


def mm_exact(left, right):
    return jnp.dot(left, right, precision=lax.Precision.HIGHEST, preferred_element_type=F32)


def silu(values):
    return values / (1.0 + jnp.exp(-values))


def unit_inverses(lowers, masks, eye):
    span = lowers[0].shape[0]
    inverses = [eye - lower * masks[0] for lower in lowers]
    level, size = 1, 2
    while size < span:
        mask = masks[level]
        if size < RIM:
            steps = [mm(low * mask, inv).astype(BF16) for low, inv in zip(lowers, inverses)]
            news = [mm(inv, step).astype(BF16) for inv, step in zip(inverses, steps)]
            inverses = [inv - new for inv, new in zip(inverses, news)]
        else:
            cuts = [slice(at, at + size) for at in range(0, span, size)]

            def odd(values):
                return jnp.concatenate([values[cut] for cut in cuts[1::2]], axis=0)

            odd_mask = odd(mask)
            halves = [mm(odd(low) * odd_mask, inv).astype(BF16) for low, inv in zip(lowers, inverses)]
            gap = jnp.zeros((size, span), BF16)
            steps = [
                jnp.concatenate(
                    [part for at in range(0, span // 2, size) for part in (gap, half[at : at + size])],
                    axis=0,
                )
                for half in halves
            ]
            odds = [odd(inv) for inv in inverses]
            news = [own - mm(own, step).astype(BF16) for own, step in zip(odds, steps)]
            inverses = [
                jnp.concatenate(
                    [
                        part
                        for i, cut in enumerate(cuts[0::2])
                        for part in (inv[cut], new[i * size : (i + 1) * size])
                    ],
                    axis=0,
                )
                for inv, new in zip(inverses, news)
            ]
        level, size = level + 1, 2 * size
    return inverses


def largest(count, most):
    while count % most:
        most -= 1
    return most


def layer_kernel(
    n_ctx,
    n_head,
    q_hbm,
    k_hbm,
    v_hbm,
    qk_taps_hbm,
    v_taps_hbm,
    gate_hbm,
    beta_hbm,
    rate_hbm,
    log_rate_hbm,
    gain_hbm,
    w_hbm,
    out_ref,
    q_ref,
    k_ref,
    v_ref,
    qk_taps_ref,
    v_taps_ref,
    gate_ref,
    beta_ref,
    rate_ref,
    log_rate_ref,
    gain_ref,
    w_ref,
    in_sem,
    ext,
    rim_q,
    rim_k,
    rim_v,
    taps,
    square,
    masks_ref,
    gamma_rows,
    beta_rows,
    map_ref,
    push_ref,
    lift_ref,
    local_ref,
    last_ref,
    state_in,
    state_out,
    gates,
    total,
    part,
    part_in,
    rim_send,
    rim_recv,
    state_send,
    state_recv,
    part_send,
    part_recv,
):
    ctx = lax.axis_index("ctx")
    head = lax.axis_index("head")
    length = q_ref.shape[0]
    qk_width = q_ref.shape[1]
    v_width = v_ref.shape[1]
    heads = v_width // HDIM
    ratio = v_width // qk_width
    rows_out = length // n_head
    chunks, _, chunk_width = part.shape
    has_next = ctx < n_ctx - 1
    has_prev = ctx > 0
    early = ctx < n_ctx // 2
    after = jnp.minimum(ctx + 1, n_ctx - 1)
    before = jnp.maximum(ctx - 1, 0)

    barrier = pltpu.get_barrier_semaphore()

    @pl.when(has_next)
    def _():
        pl.semaphore_signal(barrier, inc=1, device_id=(after, head), device_id_type=MESH)

    @pl.when(has_prev)
    def _():
        pl.semaphore_signal(barrier, inc=1, device_id=(before, head), device_id_type=MESH)

    for hop in range(1, n_head):
        peer = lax.rem(head + hop, n_head)
        pl.semaphore_signal(barrier, inc=1, device_id=(ctx, peer), device_id_type=MESH)

    ins = [
        pltpu.make_async_copy(src, dst, in_sem.at[i])
        for i, (src, dst) in enumerate(
            (
                (rate_hbm, rate_ref),
                (log_rate_hbm, log_rate_ref),
                (beta_hbm, beta_ref),
                (qk_taps_hbm, qk_taps_ref),
                (v_taps_hbm, v_taps_ref),
                (q_hbm, q_ref),
                (k_hbm, k_ref),
                (v_hbm, v_ref),
                (gain_hbm, gain_ref),
                (gate_hbm, gate_ref),
                (w_hbm, w_ref),
            )
        )
    ]
    for copy in ins:
        copy.start()

    neighbours = has_next.astype(jnp.int32) + has_prev.astype(jnp.int32) + (n_head - 1)
    pl.semaphore_wait(barrier, neighbours)

    rims = [
        pltpu.make_async_remote_copy(
            src_ref=src.at[pl.ds(length - RIM, RIM), :],
            dst_ref=dst,
            send_sem=rim_send.at[i],
            recv_sem=rim_recv.at[i],
            device_id=(after, head),
            device_id_type=MESH,
        )
        for i, (src, dst) in enumerate(((q_hbm, rim_q), (k_hbm, rim_k), (v_hbm, rim_v)))
    ]

    @pl.when(has_next)
    def _():
        for copy in rims:
            copy.start()

    row = lax.broadcasted_iota(jnp.int32, (HDIM, HDIM), 0)
    col = lax.broadcasted_iota(jnp.int32, (HDIM, HDIM), 1)
    size = 1
    for level in range(masks_ref.shape[0]):
        inside = (row // (2 * size) == col // (2 * size)) & (row // size > col // size)
        masks_ref[level] = jnp.where(inside, 1.0, 0.0).astype(BF16)
        size *= 2
    for copy in ins[0:3]:
        copy.wait()
    rate = rate_ref[...]
    soft = jnp.maximum(rate, 0.0) + jnp.log1p(jnp.exp(-jnp.abs(rate)))
    square[...] = jnp.zeros_like(square)
    square[:, 0:heads] = jnp.broadcast_to(log_rate_ref[...], (HDIM, heads))
    decay = -jnp.exp(square[...].T[0:heads]) * soft
    upper = jnp.where(row <= col, 1.0, 0.0)
    gamma_rows[...] = mm_exact(decay, upper)
    beta_rows[...] = 1.0 / (1.0 + jnp.exp(-beta_ref[...]))
    for copy in ins[3:8]:
        copy.wait()
    taps[:, 0:qk_width] = qk_taps_ref[0].astype(F32)
    taps[:, qk_width : 2 * qk_width] = qk_taps_ref[1].astype(F32)
    taps[:, 2 * qk_width :] = v_taps_ref[...].astype(F32)
    spans = ((q_ref, rim_q, 0), (k_ref, rim_k, qk_width), (v_ref, rim_v, 2 * qk_width))
    for ref, _, start in spans:
        ext[8 : 8 + length, start : start + ref.shape[1]] = ref[...].astype(F32)

    @pl.when(has_prev)
    def _():
        for copy in rims:
            copy.wait_recv()
        for _, rim, start in spans:
            ext[0:8, start : start + rim.shape[1]] = rim[...].astype(F32)[RIM - 8 : RIM]

    @pl.when(jnp.logical_not(has_prev))
    def _():
        ext[0:8, :] = jnp.zeros((8, ext.shape[1]), F32)
        state_in[...] = jnp.zeros_like(state_in)

    def conv(start):
        at = pl.ds(pl.multiple_of(start, HDIM), HDIM)
        result = taps[0:1, at] * ext[5 : 5 + length, at]
        for offset in range(1, CONV):
            result += taps[offset : offset + 1, at] * ext[5 + offset : 5 + offset + length, at]
        return silu(result)

    def unit(values):
        return values * lax.rsqrt(jnp.sum(values * values, axis=-1, keepdims=True) + 1e-06)

    key_heads = heads // ratio
    key_group = largest(key_heads, 4)

    def local_step(group, _):
        owns = [group * key_group + i for i in range(key_group)]
        queries = [unit(conv(own * HDIM)) * HDIM ** (-0.5) for own in owns]
        keys = [unit(conv(qk_width + own * HDIM)) for own in owns]
        keys_t = [key.T for key in keys]
        key_keys = [mm(key, key_t) for key, key_t in zip(keys, keys_t)]
        query_keys = [mm(query, key_t) for query, key_t in zip(queries, keys_t)]
        upto = row >= col
        lowers, scores, rights, lifts, tails = [], [], [], [], []
        for i in range(key_group * ratio):
            h, k = group * (key_group * ratio) + i, i // ratio
            gamma_r = gamma_rows[pl.ds(h, 1), :]
            beta_r = beta_rows[pl.ds(h, 1), :]
            gamma_c = jnp.broadcast_to(gamma_r, (HDIM, HDIM)).T
            faded = jnp.exp(jnp.where(upto, gamma_c - gamma_r, 0.0)) * beta_r
            lowers.append(jnp.where(row > col, faded * key_keys[k], 0.0).astype(BF16))
            scores.append(jnp.where(upto, faded * query_keys[k], 0.0).astype(BF16))
            growth = jnp.exp(gamma_c)
            last = gamma_c[HDIM - 1 : HDIM, :]
            value = conv(2 * qk_width + h * HDIM)
            rights.append(jnp.concatenate([value, growth * keys[k]], axis=1).astype(BF16))
            lifts.append(growth * queries[k])
            tails.append((keys_t[k] * (jnp.exp(last - gamma_r) * beta_r)).astype(BF16))
            last_ref[pl.ds(h, 1), :] = jnp.exp(last)
        eye = jnp.where(row == col, 1.0, 0.0).astype(BF16)
        masks = [masks_ref[level] for level in range(masks_ref.shape[0])]
        inverses = unit_inverses(lowers, masks, eye)
        solved = [mm(inv, right).astype(BF16) for inv, right in zip(inverses, rights)]
        pushes = [mm(tail, one) for tail, one in zip(tails, solved)]
        raises = [mm(score, one) for score, one in zip(scores, solved)]
        for i in range(key_group * ratio):
            h = group * (key_group * ratio) + i
            map_ref[h] = pushes[i][:, HDIM:].astype(BF16)
            push_ref[h] = pushes[i][:, :HDIM]
            lift_ref[h] = (lifts[i] - raises[i][:, HDIM:]).astype(BF16)
            local_ref[h] = raises[i][:, :HDIM]
        return 0

    lax.fori_loop(0, key_heads // key_group, local_step, 0)

    def state_copy(h):
        return pltpu.make_async_remote_copy(
            src_ref=state_out.at[h],
            dst_ref=state_in.at[h],
            send_sem=state_send.at[h],
            recv_sem=state_recv.at[h],
            device_id=(after, head),
            device_id_type=MESH,
        )

    def forward(h):
        @pl.when(has_prev)
        def _():
            state_copy(h).wait_recv()

        @pl.when(has_next)
        def _():
            arrived = state_in[h]
            moved = jnp.dot(map_ref[h], arrived, preferred_element_type=F32)
            grown = last_ref[pl.ds(h, 1), :] * arrived.astype(F32)
            state_out[h] = (grown - moved + push_ref[h]).astype(BF16)
            state_copy(h).start()

    @pl.when(early)
    def _():
        def all_forward(h, _):
            forward(h)
            return 0

        lax.fori_loop(0, heads, all_forward, 0)

    for copy in ins[8:11]:
        copy.wait()

    def open_gate(h, _):
        at = pl.ds(pl.multiple_of(h * HDIM, HDIM), HDIM)
        gates[:, at] = gain_ref[...] * silu(gate_ref[:, at].astype(F32))
        return 0

    lax.fori_loop(0, heads, open_gate, 0)

    sweep_group = largest(heads, 4)
    sweeps = heads // sweep_group
    depth = sweep_group * HDIM

    def normed_group(group):
        first = group * sweep_group

        @pl.when(jnp.logical_not(early))
        def _():
            for i in range(sweep_group):
                forward(first + i)

        cores = [
            local_ref[first + i]
            + jnp.dot(lift_ref[first + i], state_in[first + i], preferred_element_type=F32)
            for i in range(sweep_group)
        ]
        scales = [lax.rsqrt(jnp.mean(core * core, axis=-1, keepdims=True) + 1e-06) for core in cores]
        normed = [
            core * scale * gates[:, pl.ds(pl.multiple_of((first + i) * HDIM, HDIM), HDIM)]
            for i, (core, scale) in enumerate(zip(cores, scales))
        ]
        return jnp.concatenate(normed, axis=1).astype(BF16)

    def product(normed, group, chunk):
        rows = pl.ds(pl.multiple_of(group * depth, depth), depth)
        weight = w_ref[rows, chunk * chunk_width : (chunk + 1) * chunk_width]
        return jnp.dot(normed, weight, preferred_element_type=F32)

    total[...] = jnp.zeros_like(total)

    def sweep(group, _):
        normed = normed_group(group)
        for chunk in range(chunks):
            total[chunk] += product(normed, group, chunk)
        return 0

    lax.fori_loop(0, sweeps - 1, sweep, 0)

    normed = normed_group(sweeps - 1)
    copies = []
    for chunk in range(chunks):
        part[chunk] = (total[chunk] + product(normed, sweeps - 1, chunk)).astype(BF16)
        for hop in range(1, n_head):
            peer = lax.rem(head + hop, n_head)
            copy = pltpu.make_async_remote_copy(
                src_ref=part.at[chunk, pl.ds(pl.multiple_of(peer * rows_out, 16), rows_out), :],
                dst_ref=part_in.at[hop - 1, chunk],
                send_sem=part_send.at[hop - 1, chunk],
                recv_sem=part_recv.at[hop - 1, chunk],
                device_id=(ctx, peer),
                device_id_type=MESH,
            )
            copy.start()
            copies.append((chunk, hop - 1, copy))
    kept = pl.ds(pl.multiple_of(head * rows_out, 16), rows_out)
    for chunk in range(chunks):
        mixed = part[chunk, kept, :].astype(F32)
        for own, hop, copy in copies:
            if own == chunk:
                copy.wait_recv()
                mixed += part_in[hop, chunk].astype(F32)
        out_ref[:, chunk * chunk_width : (chunk + 1) * chunk_width] = mixed.astype(BF16)

    for _, _, copy in copies:
        copy.wait_send()

    @pl.when(has_next)
    def _():
        for copy in rims:
            copy.wait_send()

        def drain(h, _):
            state_copy(h).wait_send()
            return 0

        lax.fori_loop(0, heads, drain, 0)


def local(n_ctx, n_head, *args):
    (q, k, v, qk_taps, v_taps, gate, beta, rate, log_rate, gain, weight) = args
    length, qk_width = q.shape
    v_width = v.shape[1]
    heads = v_width // HDIM
    model = weight.shape[1]
    rows_out = length // n_head
    width = 2 * qk_width + v_width
    dma = pltpu.SemaphoreType.DMA
    blocks = (heads, HDIM, HDIM)
    peers = max(n_head - 1, 1)
    chunks = 4
    operands = (
        q, k, v, qk_taps, v_taps, gate, beta.T, rate.T, log_rate[None, :], gain[None, :], weight
    )
    return pl.pallas_call(
        functools.partial(layer_kernel, n_ctx, n_head),
        out_shape=jax.ShapeDtypeStruct((rows_out, model), BF16),
        in_specs=[pl.BlockSpec(memory_space=pl.ANY)] * len(operands),
        out_specs=pl.BlockSpec(memory_space=pltpu.VMEM),
        scratch_shapes=[
            *[pltpu.VMEM(operand.shape, operand.dtype) for operand in operands],
            dma((len(operands),)),
            pltpu.VMEM((8 + length, width), F32),
            pltpu.VMEM((RIM, qk_width), BF16),
            pltpu.VMEM((RIM, qk_width), BF16),
            pltpu.VMEM((RIM, v_width), BF16),
            pltpu.VMEM((CONV, width), F32),
            pltpu.VMEM((HDIM, HDIM), F32),
            pltpu.VMEM((HDIM.bit_length() - 1, HDIM, HDIM), BF16),
            pltpu.VMEM((heads, HDIM), F32),
            pltpu.VMEM((heads, HDIM), F32),
            pltpu.VMEM(blocks, BF16),
            pltpu.VMEM(blocks, F32),
            pltpu.VMEM(blocks, BF16),
            pltpu.VMEM(blocks, F32),
            pltpu.VMEM((heads, HDIM), F32),
            pltpu.VMEM(blocks, BF16),
            pltpu.VMEM(blocks, BF16),
            pltpu.VMEM((length, v_width), F32),
            pltpu.VMEM((chunks, length, model // chunks), F32),
            pltpu.VMEM((chunks, length, model // chunks), BF16),
            pltpu.VMEM((peers, chunks, rows_out, model // chunks), BF16),
            dma((3,)),
            dma((3,)),
            dma((heads,)),
            dma((heads,)),
            dma((peers, chunks)),
            dma((peers, chunks)),
        ],
        compiler_params=pltpu.CompilerParams(
            collective_id=0, has_side_effects=True, vmem_limit_bytes=60 * 2**20
        ),
    )(*operands)


def solution(mesh):
    in_specs = (
        P("ctx", "head"),
        P("ctx", "head"),
        P("ctx", "head"),
        P(None, None, "head"),
        P(None, "head"),
        P("ctx", "head"),
        P("ctx", "head"),
        P("ctx", "head"),
        P("head"),
        P(),
        P("head", None),
    )
    out_specs = P(("ctx", "head"), None)
    return jax.shard_map(
        functools.partial(local, mesh.shape["ctx"], mesh.shape["head"]),
        mesh=mesh,
        in_specs=in_specs,
        out_specs=out_specs,
        check_vma=False,
    )
```

time: 84.2 us -> 52.3 us (0.62)
  Pallas kernels: 74.7 us -> 50.4 us
  local copies, waits for them, and re-layouts: 9.02 us -> 1.67 us
    pallas_call x1, Pallas kernels: 74.7 us -> 50.4 us  [local(): pl.pallas_call(functools.partial(layer_kernel, n_ctx, n_head), out_shape=...]
    unnamed x19 -> x1, local copies, waits for them, and re-layouts: 9.02 us -> 1.67 us
where the time goes in v2:
time: 52.3 us; the launch traced here: 52.1 us
  Pallas kernels  50.4 us (96%)
  local copies, waits for them, and re-layouts  1.67 us (3%)
    pallas_call x1, Pallas kernels, local(): pl.pallas_call(functools.partial(layer_kernel, n_ctx, n_head), out_shape=...  50.4 us
    unnamed x1, local copies, waits for them, and re-layouts  1.67 us

profile of v2, /device:TPU:27, one launch (start us, length us, event | category | flops | bytes accessed | tf_op | source)
XLA Modules:
  0.0 52.1 jit_solution(2483266622054814633)
XLA Ops:
  0.0 50.4 %shard_map.109 = bf16[64,2048]{1,0:T(8,128)(2,1)} custom-call(bf16[128,1024]{1,0:T(8,128)(2,1)} %q_hbm.1, bf16[128,1024]{1,0:T(8,128)(2,1)} %k_hbm.1, bf16[128,2048]{1,0:T(8,128)(2,1)} %v_hbm.1, bf16[2,4,1024]{2,1,0:T(4,128)(2,1)} %qk_taps_hbm.1, bf16[4,2048]{1,0:T(4,128)(2,1)} %v_taps_hbm.1, bf16[128,2048]{1,0:T(8,128)(2,1)} %gate_hbm.1, ...), custom_call_target="tpu_custom_call" | custom-call | tf_op jit(solution)/shard_map/pallas_call | solution.py:429
  50.4 1.7 %copy.13 = bf16[64,2048]{1,0:T(8,128)(2,1)} copy(bf16[64,2048]{1,0:T(8,128)(2,1)} %shard_map.109) | data formatting | bytes 524288

commit v3 on v2

--- a/solution.py
+++ b/solution.py
@@ -10,6 +10,7 @@
 HDIM = 128
 CONV = 4
 RIM = 16
+PLANE = 4
 MESH = pl.DeviceIdType.MESH
 F32 = jnp.float32
 BF16 = jnp.bfloat16
@@ -113,20 +114,31 @@
     gamma_rows,
     beta_rows,
     map_ref,
-    push_ref,
+    near_map,
+    joined_out,
+    joined_in,
     lift_ref,
     local_ref,
-    last_ref,
+    entry,
+    entry_out,
     state_in,
-    state_out,
+    mate_out,
     gates,
     total,
     part,
     part_in,
     rim_send,
     rim_recv,
-    state_send,
-    state_recv,
+    near_send,
+    near_recv,
+    joined_send,
+    joined_recv,
+    entry_send,
+    entry_recv,
+    fan_send,
+    fan_recv,
+    mate_send,
+    mate_recv,
     part_send,
     part_recv,
 ):
@@ -141,19 +153,34 @@
     chunks, _, chunk_width = part.shape
     has_next = ctx < n_ctx - 1
     has_prev = ctx > 0
-    early = ctx < n_ctx // 2
-    after = jnp.minimum(ctx + 1, n_ctx - 1)
-    before = jnp.maximum(ctx - 1, 0)
+    place = lax.rem(ctx, PLANE)
+    is_even = lax.rem(place, 2) == 0
+    is_joiner = place == 1
+    is_chain = place == PLANE - 1
+    chain_next = is_chain & (ctx + PLANE < n_ctx)
+    chain_prev = is_chain & (ctx >= PLANE)
+
+    def at(offset):
+        return (jnp.clip(ctx + offset, 0, n_ctx - 1), head)
+
+    links = (
+        (1, has_next),
+        (-1, has_prev),
+        (2, is_joiner),
+        (-2, is_chain),
+        (PLANE, chain_next),
+        (-PLANE, chain_prev),
+    )
 
     barrier = pltpu.get_barrier_semaphore()
 
-    @pl.when(has_next)
-    def _():
-        pl.semaphore_signal(barrier, inc=1, device_id=(after, head), device_id_type=MESH)
-
-    @pl.when(has_prev)
-    def _():
-        pl.semaphore_signal(barrier, inc=1, device_id=(before, head), device_id_type=MESH)
+    neighbours = n_head - 1
+    for offset, there in links:
+        neighbours += there.astype(jnp.int32)
+
+        @pl.when(there)
+        def _(offset=offset):
+            pl.semaphore_signal(barrier, inc=1, device_id=at(offset), device_id_type=MESH)
 
     for hop in range(1, n_head):
         peer = lax.rem(head + hop, n_head)
@@ -180,7 +207,6 @@
     for copy in ins:
         copy.start()
 
-    neighbours = has_next.astype(jnp.int32) + has_prev.astype(jnp.int32) + (n_head - 1)
     pl.semaphore_wait(barrier, neighbours)
 
     rims = [
@@ -189,7 +215,7 @@
             dst_ref=dst,
             send_sem=rim_send.at[i],
             recv_sem=rim_recv.at[i],
-            device_id=(after, head),
+            device_id=at(1),
             device_id_type=MESH,
         )
         for i, (src, dst) in enumerate(((q_hbm, rim_q), (k_hbm, rim_k), (v_hbm, rim_v)))
@@ -236,13 +262,36 @@
     @pl.when(jnp.logical_not(has_prev))
     def _():
         ext[0:8, :] = jnp.zeros((8, ext.shape[1]), F32)
-        state_in[...] = jnp.zeros_like(state_in)
+
+    @pl.when(is_chain & jnp.logical_not(chain_prev))
+    def _():
+        entry[...] = jnp.zeros_like(entry)
+
+    def per_head(src, dst, send, recv, offset):
+        def copy_of(h):
+            return pltpu.make_async_remote_copy(
+                src_ref=src.at[h],
+                dst_ref=dst.at[h],
+                send_sem=send.at[h],
+                recv_sem=recv.at[h],
+                device_id=at(offset),
+                device_id_type=MESH,
+            )
+
+        return copy_of
+
+    near_copy = per_head(map_ref, near_map, near_send, near_recv, 1)
+    joined_copy = per_head(joined_out, joined_in, joined_send, joined_recv, 2)
+    entry_copy = per_head(entry_out, entry, entry_send, entry_recv, PLANE)
+    fan_copy = per_head(entry, entry, fan_send, fan_recv, -2)
+    mate_copy = per_head(mate_out, state_in, mate_send, mate_recv, -1)
+    relay_copy = per_head(entry, state_in, mate_send, mate_recv, -1)
 
     def conv(start):
-        at = pl.ds(pl.multiple_of(start, HDIM), HDIM)
-        result = taps[0:1, at] * ext[5 : 5 + length, at]
+        lanes = pl.ds(pl.multiple_of(start, HDIM), HDIM)
+        result = taps[0:1, lanes] * ext[5 : 5 + length, lanes]
         for offset in range(1, CONV):
-            result += taps[offset : offset + 1, at] * ext[5 + offset : 5 + offset + length, at]
+            result += taps[offset : offset + 1, lanes] * ext[5 + offset : 5 + offset + length, lanes]
         return silu(result)
 
     def unit(values):
@@ -259,7 +308,7 @@
         key_keys = [mm(key, key_t) for key, key_t in zip(keys, keys_t)]
         query_keys = [mm(query, key_t) for query, key_t in zip(queries, keys_t)]
         upto = row >= col
-        lowers, scores, rights, lifts, tails = [], [], [], [], []
+        lowers, scores, rights, lifts, tails, lasts = [], [], [], [], [], []
         for i in range(key_group * ratio):
             h, k = group * (key_group * ratio) + i, i // ratio
             gamma_r = gamma_rows[pl.ds(h, 1), :]
@@ -274,7 +323,7 @@
             rights.append(jnp.concatenate([value, growth * keys[k]], axis=1).astype(BF16))
             lifts.append(growth * queries[k])
             tails.append((keys_t[k] * (jnp.exp(last - gamma_r) * beta_r)).astype(BF16))
-            last_ref[pl.ds(h, 1), :] = jnp.exp(last)
+            lasts.append(jnp.exp(last))
         eye = jnp.where(row == col, 1.0, 0.0).astype(BF16)
         masks = [masks_ref[level] for level in range(masks_ref.shape[0])]
         inverses = unit_inverses(lowers, masks, eye)
@@ -283,54 +332,80 @@
         raises = [mm(score, one) for score, one in zip(scores, solved)]
         for i in range(key_group * ratio):
             h = group * (key_group * ratio) + i
-            map_ref[h] = pushes[i][:, HDIM:].astype(BF16)
-            push_ref[h] = pushes[i][:, :HDIM]
+            kept = jnp.where(row == col, lasts[i], 0.0) - pushes[i][:, HDIM:]
+            map_ref[h] = jnp.concatenate([kept, pushes[i][:, :HDIM]], axis=1).astype(BF16)
             lift_ref[h] = (lifts[i] - raises[i][:, HDIM:]).astype(BF16)
             local_ref[h] = raises[i][:, :HDIM]
+        first = group * (key_group * ratio)
+
+        @pl.when(is_even)
+        def _():
+            for i in range(key_group * ratio):
+                near_copy(first + i).start()
+
+        @pl.when(is_joiner)
+        def _():
+            for i in range(key_group * ratio):
+                near_copy(first + i).wait_recv()
+            for i in range(key_group * ratio):
+                own = map_ref[first + i]
+                moved = mm(own[:, :HDIM], near_map[first + i])
+                push = moved[:, HDIM:] + own[:, HDIM:].astype(F32)
+                joined_out[first + i] = jnp.concatenate([moved[:, :HDIM], push], axis=1).astype(BF16)
+                joined_copy(first + i).start()
+
         return 0
 
     lax.fori_loop(0, key_heads // key_group, local_step, 0)
 
-    def state_copy(h):
-        return pltpu.make_async_remote_copy(
-            src_ref=state_out.at[h],
-            dst_ref=state_in.at[h],
-            send_sem=state_send.at[h],
-            recv_sem=state_recv.at[h],
-            device_id=(after, head),
-            device_id_type=MESH,
-        )
-
-    def forward(h):
-        @pl.when(has_prev)
-        def _():
-            state_copy(h).wait_recv()
-
-        @pl.when(has_next)
-        def _():
-            arrived = state_in[h]
-            moved = jnp.dot(map_ref[h], arrived, preferred_element_type=F32)
-            grown = last_ref[pl.ds(h, 1), :] * arrived.astype(F32)
-            state_out[h] = (grown - moved + push_ref[h]).astype(BF16)
-            state_copy(h).start()
-
-    @pl.when(early)
-    def _():
-        def all_forward(h, _):
-            forward(h)
-            return 0
-
-        lax.fori_loop(0, heads, all_forward, 0)
+    def apply(pair, state):
+        return (mm(pair[:, :HDIM], state) + pair[:, HDIM:].astype(F32)).astype(BF16)
 
     for copy in ins[8:11]:
         copy.wait()
 
     def open_gate(h, _):
-        at = pl.ds(pl.multiple_of(h * HDIM, HDIM), HDIM)
-        gates[:, at] = gain_ref[...] * silu(gate_ref[:, at].astype(F32))
+        lanes = pl.ds(pl.multiple_of(h * HDIM, HDIM), HDIM)
+        gates[:, lanes] = gain_ref[...] * silu(gate_ref[:, lanes].astype(F32))
         return 0
 
     lax.fori_loop(0, heads, open_gate, 0)
+    total[...] = jnp.zeros_like(total)
+
+    @pl.when(is_chain)
+    def _():
+        def step(pair, _):
+            both = (2 * pair, 2 * pair + 1)
+            for h in both:
+                near_copy(h).wait_recv()
+                joined_copy(h).wait_recv()
+
+            @pl.when(chain_prev)
+            def _():
+                for h in both:
+                    entry_copy(h).wait_recv()
+
+            for h in both:
+                fan_copy(h).start()
+            seconds = [apply(joined_in[h], entry[h]) for h in both]
+            for h, second in zip(both, seconds):
+                mate_out[h] = second
+            thirds = [apply(near_map[h], second) for h, second in zip(both, seconds)]
+            for h, third in zip(both, thirds):
+                state_in[h] = third
+
+            @pl.when(chain_next)
+            def _():
+                for h in both:
+                    entry_out[h] = apply(map_ref[h], state_in[h])
+                for h in both:
+                    entry_copy(h).start()
+
+            for h in both:
+                mate_copy(h).start()
+            return 0
+
+        lax.fori_loop(0, heads // 2, step, 0)
 
     sweep_group = largest(heads, 4)
     sweeps = heads // sweep_group
@@ -339,10 +414,18 @@
     def normed_group(group):
         first = group * sweep_group
 
-        @pl.when(jnp.logical_not(early))
+        @pl.when(is_even)
         def _():
             for i in range(sweep_group):
-                forward(first + i)
+                mate_copy(first + i).wait_recv()
+
+        @pl.when(is_joiner)
+        def _():
+            for i in range(sweep_group):
+                fan_copy(first + i).wait_recv()
+                relay_copy(first + i).start()
+            for i in range(sweep_group):
+                state_in[first + i] = apply(near_map[first + i], entry[first + i])
 
         cores = [
             local_ref[first + i]
@@ -360,8 +443,6 @@
         rows = pl.ds(pl.multiple_of(group * depth, depth), depth)
         weight = w_ref[rows, chunk * chunk_width : (chunk + 1) * chunk_width]
         return jnp.dot(normed, weight, preferred_element_type=F32)
-
-    total[...] = jnp.zeros_like(total)
 
     def sweep(group, _):
         normed = normed_group(group)
@@ -404,11 +485,23 @@
         for copy in rims:
             copy.wait_send()
 
-        def drain(h, _):
-            state_copy(h).wait_send()
-            return 0
-
-        lax.fori_loop(0, heads, drain, 0)
+    sent = (
+        (near_copy, is_even),
+        (joined_copy, is_joiner),
+        (relay_copy, is_joiner),
+        (entry_copy, chain_next),
+        (fan_copy, is_chain),
+        (mate_copy, is_chain),
+    )
+    for copy_of, mine in sent:
+
+        @pl.when(mine)
+        def _(copy_of=copy_of):
+            def drain(h, _):
+                copy_of(h).wait_send()
+                return 0
+
+            lax.fori_loop(0, heads, drain, 0)
 
 
 def local(n_ctx, n_head, *args):
@@ -443,21 +536,17 @@
             pltpu.VMEM((HDIM.bit_length() - 1, HDIM, HDIM), BF16),
             pltpu.VMEM((heads, HDIM), F32),
             pltpu.VMEM((heads, HDIM), F32),
+            *[pltpu.VMEM((heads, HDIM, 2 * HDIM), BF16)] * 4,
             pltpu.VMEM(blocks, BF16),
             pltpu.VMEM(blocks, F32),
-            pltpu.VMEM(blocks, BF16),
-            pltpu.VMEM(blocks, F32),
-            pltpu.VMEM((heads, HDIM), F32),
-            pltpu.VMEM(blocks, BF16),
-            pltpu.VMEM(blocks, BF16),
+            *[pltpu.VMEM(blocks, BF16)] * 4,
             pltpu.VMEM((length, v_width), F32),
             pltpu.VMEM((chunks, length, model // chunks), F32),
             pltpu.VMEM((chunks, length, model // chunks), BF16),
             pltpu.VMEM((peers, chunks, rows_out, model // chunks), BF16),
             dma((3,)),
             dma((3,)),
-            dma((heads,)),
-            dma((heads,)),
+            *[dma((heads,))] * 10,
             dma((peers, chunks)),
             dma((peers, chunks)),
         ],

time: 52.3 us -> 43.7 us (0.84)
  the two profiles are of different devices: /device:TPU:27 before, /device:TPU:24 now
where the time goes in v3:
time: 43.7 us; the launch traced here: 43.6 us
  Pallas kernels  41.9 us (96%)
  local copies, waits for them, and re-layouts  1.67 us (4%)
    pallas_call x1, Pallas kernels, local(): pl.pallas_call(functools.partial(layer_kernel, n_ctx, n_head), out_shape=...  41.9 us
    unnamed x1, local copies, waits for them, and re-layouts  1.67 us

profile of v3, /device:TPU:24, one launch (start us, length us, event | category | flops | bytes accessed | tf_op | source)
XLA Modules:
  0.0 43.6 jit_solution(10305364875060323211)
XLA Ops:
  0.0 41.9 %shard_map.109 = bf16[64,2048]{1,0:T(8,128)(2,1)} custom-call(bf16[128,1024]{1,0:T(8,128)(2,1)} %q_hbm.1, bf16[128,1024]{1,0:T(8,128)(2,1)} %k_hbm.1, bf16[128,2048]{1,0:T(8,128)(2,1)} %v_hbm.1, bf16[2,4,1024]{2,1,0:T(4,128)(2,1)} %qk_taps_hbm.1, bf16[4,2048]{1,0:T(4,128)(2,1)} %v_taps_hbm.1, bf16[128,2048]{1,0:T(8,128)(2,1)} %gate_hbm.1, ...), custom_call_target="tpu_custom_call" | custom-call | tf_op jit(solution)/shard_map/pallas_call | solution.py:522
  41.9 1.7 %copy.13 = bf16[64,2048]{1,0:T(8,128)(2,1)} copy(bf16[64,2048]{1,0:T(8,128)(2,1)} %shard_map.109) | data formatting | bytes 524288

commit v4 on v3

--- a/solution.py
+++ b/solution.py
@@ -155,10 +155,14 @@
     has_prev = ctx > 0
     place = lax.rem(ctx, PLANE)
     is_even = lax.rem(place, 2) == 0
-    is_joiner = place == 1
-    is_chain = place == PLANE - 1
-    chain_next = is_chain & (ctx + PLANE < n_ctx)
-    chain_prev = is_chain & (ctx >= PLANE)
+    is_odd = jnp.logical_not(is_even)
+    is_mid = place == 1
+    is_end = place == PLANE - 1
+    chain_next = is_odd & (ctx + PLANE < n_ctx)
+    chain_prev = is_odd & (ctx >= PLANE)
+    other = 4 - 2 * place
+    chain_base = jnp.where(is_mid, 2, 0)
+    relay_base = 2 - chain_base
 
     def at(offset):
         return (jnp.clip(ctx + offset, 0, n_ctx - 1), head)
@@ -166,8 +170,7 @@
     links = (
         (1, has_next),
         (-1, has_prev),
-        (2, is_joiner),
-        (-2, is_chain),
+        (other, is_odd),
         (PLANE, chain_next),
         (-PLANE, chain_prev),
     )
@@ -263,9 +266,14 @@
     def _():
         ext[0:8, :] = jnp.zeros((8, ext.shape[1]), F32)
 
-    @pl.when(is_chain & jnp.logical_not(chain_prev))
-    def _():
-        entry[...] = jnp.zeros_like(entry)
+    @pl.when(is_odd & jnp.logical_not(chain_prev))
+    def _():
+        def clear(four, _):
+            for j in range(2):
+                entry[4 * four + chain_base + j] = jnp.zeros((HDIM, HDIM), BF16)
+            return 0
+
+        lax.fori_loop(0, heads // 4, clear, 0)
 
     def per_head(src, dst, send, recv, offset):
         def copy_of(h):
@@ -281,9 +289,10 @@
         return copy_of
 
     near_copy = per_head(map_ref, near_map, near_send, near_recv, 1)
-    joined_copy = per_head(joined_out, joined_in, joined_send, joined_recv, 2)
+    joined_copy = per_head(joined_out, joined_in, joined_send, joined_recv, other)
     entry_copy = per_head(entry_out, entry, entry_send, entry_recv, PLANE)
-    fan_copy = per_head(entry, entry, fan_send, fan_recv, -2)
+    fan_copy = per_head(entry, entry, fan_send, fan_recv, other)
+    fan_made = per_head(mate_out, entry, fan_send, fan_recv, other)
     mate_copy = per_head(mate_out, state_in, mate_send, mate_recv, -1)
     relay_copy = per_head(entry, state_in, mate_send, mate_recv, -1)
 
@@ -343,16 +352,17 @@
             for i in range(key_group * ratio):
                 near_copy(first + i).start()
 
-        @pl.when(is_joiner)
+        @pl.when(is_odd)
         def _():
             for i in range(key_group * ratio):
                 near_copy(first + i).wait_recv()
-            for i in range(key_group * ratio):
-                own = map_ref[first + i]
-                moved = mm(own[:, :HDIM], near_map[first + i])
-                push = moved[:, HDIM:] + own[:, HDIM:].astype(F32)
-                joined_out[first + i] = jnp.concatenate([moved[:, :HDIM], push], axis=1).astype(BF16)
-                joined_copy(first + i).start()
+            for i in range(0, key_group * ratio, 4):
+                for h in (first + i + relay_base, first + i + relay_base + 1):
+                    own = map_ref[h]
+                    moved = mm(own[:, :HDIM], near_map[h])
+                    push = moved[:, HDIM:] + own[:, HDIM:].astype(F32)
+                    joined_out[h] = jnp.concatenate([moved[:, :HDIM], push], axis=1).astype(BF16)
+                    joined_copy(h).start()
 
         return 0
 
@@ -372,12 +382,11 @@
     lax.fori_loop(0, heads, open_gate, 0)
     total[...] = jnp.zeros_like(total)
 
-    @pl.when(is_chain)
-    def _():
-        def step(pair, _):
-            both = (2 * pair, 2 * pair + 1)
+    @pl.when(is_odd)
+    def _():
+        def step(four, _):
+            both = (4 * four + chain_base, 4 * four + chain_base + 1)
             for h in both:
-                near_copy(h).wait_recv()
                 joined_copy(h).wait_recv()
 
             @pl.when(chain_prev)
@@ -385,27 +394,51 @@
                 for h in both:
                     entry_copy(h).wait_recv()
 
-            for h in both:
-                fan_copy(h).start()
-            seconds = [apply(joined_in[h], entry[h]) for h in both]
-            for h, second in zip(both, seconds):
-                mate_out[h] = second
-            thirds = [apply(near_map[h], second) for h, second in zip(both, seconds)]
-            for h, third in zip(both, thirds):
-                state_in[h] = third
-
-            @pl.when(chain_next)
+            @pl.when(is_end)
             def _():
                 for h in both:
-                    entry_out[h] = apply(map_ref[h], state_in[h])
+                    fan_copy(h).start()
+                seconds = [apply(joined_in[h], entry[h]) for h in both]
+                for h, second in zip(both, seconds):
+                    mate_out[h] = second
+                thirds = [apply(near_map[h], second) for h, second in zip(both, seconds)]
+                for h, third in zip(both, thirds):
+                    state_in[h] = third
+
+                @pl.when(chain_next)
+                def _():
+                    for h in both:
+                        entry_out[h] = apply(map_ref[h], state_in[h])
+                    for h in both:
+                        entry_copy(h).start()
+
                 for h in both:
-                    entry_copy(h).start()
-
-            for h in both:
-                mate_copy(h).start()
+                    mate_copy(h).start()
+
+            @pl.when(is_mid)
+            def _():
+                firsts = [apply(near_map[h], entry[h]) for h in both]
+                for h, first in zip(both, firsts):
+                    state_in[h] = first
+                seconds = [apply(map_ref[h], first) for h, first in zip(both, firsts)]
+                for h, second in zip(both, seconds):
+                    mate_out[h] = second
+                for h in both:
+                    fan_made(h).start()
+
+                @pl.when(chain_next)
+                def _():
+                    for h in both:
+                        entry_out[h] = apply(joined_in[h], mate_out[h])
+                    for h in both:
+                        entry_copy(h).start()
+
+                for h in both:
+                    relay_copy(h).start()
+
             return 0
 
-        lax.fori_loop(0, heads // 2, step, 0)
+        lax.fori_loop(0, heads // 4, step, 0)
 
     sweep_group = largest(heads, 4)
     sweeps = heads // sweep_group
@@ -419,13 +452,14 @@
             for i in range(sweep_group):
                 mate_copy(first + i).wait_recv()
 
-        @pl.when(is_joiner)
+        @pl.when(is_odd)
         def _():
-            for i in range(sweep_group):
-                fan_copy(first + i).wait_recv()
-                relay_copy(first + i).start()
-            for i in range(sweep_group):
-                state_in[first + i] = apply(near_map[first + i], entry[first + i])
+            both = (first + relay_base, first + relay_base + 1)
+            for h in both:
+                fan_copy(h).wait_recv()
+                relay_copy(h).start()
+            for h in both:
+                state_in[h] = apply(near_map[h], entry[h])
 
         cores = [
             local_ref[first + i]
@@ -485,23 +519,34 @@
         for copy in rims:
             copy.wait_send()
 
-    sent = (
-        (near_copy, is_even),
-        (joined_copy, is_joiner),
-        (relay_copy, is_joiner),
-        (entry_copy, chain_next),
-        (fan_copy, is_chain),
-        (mate_copy, is_chain),
-    )
-    for copy_of, mine in sent:
-
-        @pl.when(mine)
-        def _(copy_of=copy_of):
-            def drain(h, _):
-                copy_of(h).wait_send()
-                return 0
-
-            lax.fori_loop(0, heads, drain, 0)
+    @pl.when(is_even)
+    def _():
+        def drain(h, _):
+            near_copy(h).wait_send()
+            return 0
+
+        lax.fori_loop(0, heads, drain, 0)
+
+    @pl.when(is_odd)
+    def _():
+        def drain(four, _):
+            for j in range(2):
+                joined_copy(4 * four + relay_base + j).wait_send()
+                fan_copy(4 * four + chain_base + j).wait_send()
+            for j in range(4):
+                relay_copy(4 * four + j).wait_send()
+            return 0
+
+        lax.fori_loop(0, heads // 4, drain, 0)
+
+    @pl.when(chain_next)
+    def _():
+        def drain(four, _):
+            for j in range(2):
+                entry_copy(4 * four + chain_base + j).wait_send()
+            return 0
+
+        lax.fori_loop(0, heads // 4, drain, 0)
 
 
 def local(n_ctx, n_head, *args):

time: 43.7 us -> 41.7 us (0.954)
  Pallas kernels: 41.9 us -> 39.9 us
    pallas_call x1, Pallas kernels: 41.9 us -> 39.9 us  [local(): pl.pallas_call(functools.partial(layer_kernel, n_ctx, n_head), out_shape=...]
where the time goes in v4:
time: 41.7 us; the launch traced here: 41.6 us
  Pallas kernels  39.9 us (96%)
  local copies, waits for them, and re-layouts  1.67 us (4%)
    pallas_call x1, Pallas kernels, local(): pl.pallas_call(functools.partial(layer_kernel, n_ctx, n_head), out_shape=...  39.9 us
    unnamed x1, local copies, waits for them, and re-layouts  1.67 us

profile of v4, /device:TPU:24, one launch (start us, length us, event | category | flops | bytes accessed | tf_op | source)
XLA Modules:
  0.0 41.6 jit_solution(10199439356378911493)
XLA Ops:
  0.0 39.9 %shard_map.109 = bf16[64,2048]{1,0:T(8,128)(2,1)} custom-call(bf16[128,1024]{1,0:T(8,128)(2,1)} %q_hbm.1, bf16[128,1024]{1,0:T(8,128)(2,1)} %k_hbm.1, bf16[128,2048]{1,0:T(8,128)(2,1)} %v_hbm.1, bf16[2,4,1024]{2,1,0:T(4,128)(2,1)} %qk_taps_hbm.1, bf16[4,2048]{1,0:T(4,128)(2,1)} %v_taps_hbm.1, bf16[128,2048]{1,0:T(8,128)(2,1)} %gate_hbm.1, ...), custom_call_target="tpu_custom_call" | custom-call | tf_op jit(solution)/shard_map/pallas_call | solution.py:567
  39.9 1.7 %copy.13 = bf16[64,2048]{1,0:T(8,128)(2,1)} copy(bf16[64,2048]{1,0:T(8,128)(2,1)} %shard_map.109) | data formatting | bytes 524288

commit v5 on v4

--- a/solution.py
+++ b/solution.py
@@ -307,7 +307,20 @@
         return values * lax.rsqrt(jnp.sum(values * values, axis=-1, keepdims=True) + 1e-06)
 
     key_heads = heads // ratio
-    key_group = largest(key_heads, 4)
+    key_group = largest(key_heads, 2)
+    groups = key_heads // key_group
+
+    def join(group):
+        first = group * (key_group * ratio)
+        for i in range(key_group * ratio):
+            near_copy(first + i).wait_recv()
+        for i in range(0, key_group * ratio, 4):
+            for h in (first + i + relay_base, first + i + relay_base + 1):
+                own = map_ref[h]
+                moved = mm(own[:, :HDIM], near_map[h])
+                push = moved[:, HDIM:] + own[:, HDIM:].astype(F32)
+                joined_out[h] = jnp.concatenate([moved[:, :HDIM], push], axis=1).astype(BF16)
+                joined_copy(h).start()
 
     def local_step(group, _):
         owns = [group * key_group + i for i in range(key_group)]
@@ -352,21 +365,17 @@
             for i in range(key_group * ratio):
                 near_copy(first + i).start()
 
-        @pl.when(is_odd)
+        @pl.when(is_odd & (group > 0))
         def _():
-            for i in range(key_group * ratio):
-                near_copy(first + i).wait_recv()
-            for i in range(0, key_group * ratio, 4):
-                for h in (first + i + relay_base, first + i + relay_base + 1):
-                    own = map_ref[h]
-                    moved = mm(own[:, :HDIM], near_map[h])
-                    push = moved[:, HDIM:] + own[:, HDIM:].astype(F32)
-                    joined_out[h] = jnp.concatenate([moved[:, :HDIM], push], axis=1).astype(BF16)
-                    joined_copy(h).start()
+            join(group - 1)
 
         return 0
 
-    lax.fori_loop(0, key_heads // key_group, local_step, 0)
+    lax.fori_loop(0, groups, local_step, 0)
+
+    @pl.when(is_odd)
+    def _():
+        join(groups - 1)
 
     def apply(pair, state):
         return (mm(pair[:, :HDIM], state) + pair[:, HDIM:].astype(F32)).astype(BF16)
@@ -444,6 +453,15 @@
     sweeps = heads // sweep_group
     depth = sweep_group * HDIM
 
+    def relay(group):
+        for h in (group * sweep_group + relay_base, group * sweep_group + relay_base + 1):
+            fan_copy(h).wait_recv()
+            relay_copy(h).start()
+
+    @pl.when(is_odd)
+    def _():
+        relay(0)
+
     def normed_group(group):
         first = group * sweep_group
 
@@ -455,9 +473,11 @@
         @pl.when(is_odd)
         def _():
             both = (first + relay_base, first + relay_base + 1)
-            for h in both:
-                fan_copy(h).wait_recv()
-                relay_copy(h).start()
+
+            @pl.when(group < sweeps - 1)
+            def _():
+                relay(group + 1)
+
             for h in both:
                 state_in[h] = apply(near_map[h], entry[h])
 

time: 41.7 us -> 43.6 us (1.046)
  Pallas kernels: 39.9 us -> 41.7 us
    pallas_call x1, Pallas kernels: 39.9 us -> 41.7 us  [local(): pl.pallas_call(functools.partial(layer_kernel, n_ctx, n_head), out_shape=...]
where the time goes in v5:
time: 43.6 us; the launch traced here: 43.4 us
  Pallas kernels  41.7 us (96%)
  local copies, waits for them, and re-layouts  1.67 us (4%)
    pallas_call x1, Pallas kernels, local(): pl.pallas_call(functools.partial(layer_kernel, n_ctx, n_head), out_shape=...  41.7 us
    unnamed x1, local copies, waits for them, and re-layouts  1.67 us

profile of v5, /device:TPU:24, one launch (start us, length us, event | category | flops | bytes accessed | tf_op | source)
XLA Modules:
  0.0 43.4 jit_solution(2580201845375573103)
XLA Ops:
  0.0 41.7 %shard_map.109 = bf16[64,2048]{1,0:T(8,128)(2,1)} custom-call(bf16[128,1024]{1,0:T(8,128)(2,1)} %q_hbm.1, bf16[128,1024]{1,0:T(8,128)(2,1)} %k_hbm.1, bf16[128,2048]{1,0:T(8,128)(2,1)} %v_hbm.1, bf16[2,4,1024]{2,1,0:T(4,128)(2,1)} %qk_taps_hbm.1, bf16[4,2048]{1,0:T(4,128)(2,1)} %v_taps_hbm.1, bf16[128,2048]{1,0:T(8,128)(2,1)} %gate_hbm.1, ...), custom_call_target="tpu_custom_call" | custom-call | tf_op jit(solution)/shard_map/pallas_call | solution.py:587
  41.7 1.7 %copy.13 = bf16[64,2048]{1,0:T(8,128)(2,1)} copy(bf16[64,2048]{1,0:T(8,128)(2,1)} %shard_map.109) | data formatting | bytes 524288
